TPU v7x, 32 devices: a whole 2x2x4 slice. The times are simulated.
32 devices in a mesh: dp: 2 (over core), seq: 4 (over y, x), tensor: 4 (over z).
Axes of the slice: x: 2, y: 2, z: 4, core: 2. Of those that a mesh axis runs over, the one named last changes fastest.
Arguments:
- incoming_activations: bfloat16 [2, 2048, 4096], P('dp', 'seq', 'tensor'), may hold values from -6 to 6
- objective_cotangents: bfloat16 [2, 2048, 4096], P('dp', 'seq', 'tensor'), may hold values from -400 to 400
- fixed_gating_kernel: bfloat16 [4096, 7168], P('seq', 'tensor'), may hold values from -0.09375 to 0.09375
- fixed_raising_kernel: bfloat16 [4096, 7168], P('seq', 'tensor'), may hold values from -1 to 1
- correction_narrower: bfloat16 [16, 7168], P(None, 'tensor'), may hold values from -0.0625 to 0.0625
- correction_widener: bfloat16 [16, 4096], P(None, 'tensor'), may hold values from -1.5 to 1.5
- cutoff_limits: float32 [2], replicated, may hold values from 100 to 400
Outputs:
- grad_a: float32 [16, 7168], P(None, 'tensor')
- grad_b: float32 [16, 4096], P(None, 'tensor')
All inputs are finite; a program needn't handle non-finite values.
Results may differ from a plain program's by a relative error of at most 0.0041.
Values may be sent and summed in bfloat16 or wider, within the bound.
A program may use at most 128 MiB of HBM per device.

v0:
```python
import jax
import jax.numpy as jnp
from jax import lax
from jax.sharding import PartitionSpec as P


def project(features, gate_cols, up_cols):
    gate_sum = jnp.dot(
        features,
        lax.all_gather(gate_cols, "seq", axis=0, tiled=True),
        preferred_element_type=jnp.float32,
    )
    up_sum = jnp.dot(
        features,
        lax.all_gather(up_cols, "seq", axis=0, tiled=True),
        preferred_element_type=jnp.float32,
    )
    return (gate_sum, up_sum)


def body(
    incoming_activations,
    objective_cotangents,
    fixed_gating_kernel,
    fixed_raising_kernel,
    correction_narrower,
    correction_widener,
    cutoff_limits,
):
    own = lax.axis_index("dp")
    docs = lax.axis_size("dp")
    picker = (jnp.arange(docs) == own).astype(jnp.float32)
    rows = incoming_activations.shape[1]
    rank = correction_narrower.shape[0]
    result_derivative = objective_cotangents[0]
    backward_piece = jnp.dot(
        result_derivative, correction_widener.T, preferred_element_type=jnp.float32
    )
    paired = lax.all_gather(incoming_activations, "dp", axis=0, tiled=True)
    features = lax.all_gather(paired, "tensor", axis=2, tiled=True)
    flat = features.reshape(docs * rows, features.shape[2])
    width = fixed_gating_kernel.shape[1] // docs
    gate_cols = lax.dynamic_slice_in_dim(fixed_gating_kernel, own * width, width, 1)
    up_cols = lax.dynamic_slice_in_dim(fixed_raising_kernel, own * width, width, 1)
    adapter = lax.dynamic_slice_in_dim(correction_narrower, own * width, width, 1)
    gate, up = project(flat, gate_cols, up_cols)
    inner_neurons = (jax.nn.silu(gate) * up).astype(jnp.bfloat16)
    order_portion = jnp.dot(inner_neurons, adapter.T, preferred_element_type=jnp.float32)
    back_place = (picker[:, None, None] * backward_piece[None]).reshape(docs * rows, rank)
    low_sum, back_sum = lax.psum((order_portion, back_place), ("dp", "tensor"))
    low_all = low_sum.astype(jnp.bfloat16)
    back_all = back_sum.astype(jnp.bfloat16)
    own_low = lax.dynamic_slice_in_dim(low_all, own * rows, rows, 0)
    grads_a = jnp.einsum(
        "jtr,jtf->jrf",
        back_all.reshape(docs, rows, rank),
        inner_neurons.reshape(docs, rows, width),
        preferred_element_type=jnp.float32,
    )
    grad_b = jnp.einsum("tr,td->rd", own_low, result_derivative, preferred_element_type=jnp.float32)
    grads_a, grad_b = lax.psum((grads_a, grad_b), "seq")
    squares_a = jnp.sum(grads_a * grads_a, axis=(1, 2))
    squares_b = picker * jnp.sum(grad_b * grad_b)
    squares_a, squares_b = lax.psum((squares_a, squares_b), "tensor")
    squares_a = lax.psum(squares_a, "dp")
    factor_a = cutoff_limits[0] / (jnp.sqrt(squares_a) + 0.01)
    factor_b = cutoff_limits[1] / (jnp.sqrt(squares_b) + 0.01)
    scaled_b = jnp.sum(factor_b * picker) * grad_b
    scaled_a = jnp.sum(factor_a[:, None, None] * grads_a, axis=0)
    scaled_b = lax.psum(scaled_b, "dp")
    scaled_a = lax.all_gather(scaled_a, "dp", axis=1, tiled=True)
    return (scaled_a, scaled_b)


def solution(mesh):
    in_specs = (
        P("dp", "seq", "tensor"),
        P("dp", "seq", "tensor"),
        P("seq", "tensor"),
        P("seq", "tensor"),
        P(None, "tensor"),
        P(None, "tensor"),
        P(),
    )
    out_specs = (P(None, "tensor"), P(None, "tensor"))
    return jax.shard_map(body, mesh=mesh, in_specs=in_specs, out_specs=out_specs, check_vma=False)
```

profile of v0, /device:TPU:0, one launch (start us, length us, event | category | flops | bytes accessed | tf_op | source)
XLA Modules:
  0.0 471.1 jit_solution(6397972313034810953)
XLA Ops:
  7.2 0.0 copy-start
  7.2 0.0 all-gather.7.cloned.1.call-start
  7.2 0.7 all-gather.7.cloned.1.call-update
  7.9 0.0 all-gather.11.cloned.1.call-start
  8.0 3.0 constant_dynamic-slice_fusion
  11.0 0.0 all-gather.11.cloned.1.call-update
  11.0 0.0 all-gather.9.cloned.1.call-start
  11.0 11.8 %all-gather.7.cloned.1.call-done = bf16[2,512,1024]{2,1,0:T(8,128)(2,1)} async-done(((bf16[1,512,1024]{2,1,0:T(8,128)(2,1)}), bf16[2,512,1024]{2,1,0:T(8,128)(2,1)}) %all-gather.7.cloned.1.call-update) | async-done | bytes 2097168 | tf_op jit(solution)/shard_map/all_gather | solution.py:39
  22.9 0.0 copy-start.1
  22.9 0.0 all-gather.9.cloned.1.call-update
  22.9 0.0 all-gather.5.cloned.1.call-start
  22.9 2.9 constant_dynamic-slice_fusion.1
  25.8 0.0 all-gather.5.cloned.1.call-update
  25.8 0.0 all-reduce.9.cloned.1.call-start
  25.9 0.1 broadcast_bitcast_fusion
  26.0 0.0 copy-done
  26.0 0.0 copy-done.1
  26.0 0.4 fusion.6
  26.4 78.4 %all-gather.11.cloned.1.call-done = bf16[4096,896]{1,0:T(8,128)(2,1)} async-done(((bf16[1024,896]{1,0:T(8,128)(2,1)}), bf16[4096,896]{1,0:T(8,128)(2,1)}) %all-gather.11.cloned.1.call-update) | async-done | bytes 7340048 | tf_op jit(solution)/shard_map/all_gather | solution.py:15
  104.8 151.2 %all-gather.9.cloned.1.call-done = bf16[2,512,4096]{2,1,0:T(8,128)(2,1)} async-done(((bf16[2,512,1024]{2,1,0:T(8,128)(2,1)}), bf16[2,512,4096]{2,1,0:T(8,128)(2,1)}) %all-gather.9.cloned.1.call-update) | async-done | bytes 8388624 | tf_op jit(solution)/shard_map/all_gather | solution.py:40
  256.1 13.7 %fusion.19 = f32[896,1024]{1,0:T(8,128)} fusion(bf16[4096,896]{1,0:T(8,128)(2,1)} %all-gather.11.cloned.1.call-done, bf16[1024,4096]{1,0:T(8,128)(2,1)} %bitcast.49), kind=kOutput, calls=%fused_computation.34 | convolution fusion | flops 7516192768 | bytes 19398656 | tf_op jit(solution)/shard_map/dot_general | solution.py:13
  269.7 65.2 %all-gather.5.cloned.1.call-done = bf16[4096,896]{1,0:T(8,128)(2,1)} async-done(((bf16[1024,896]{1,0:T(8,128)(2,1)}), bf16[4096,896]{1,0:T(8,128)(2,1)}) %all-gather.5.cloned.1.call-update) | async-done | bytes 7340048 | tf_op jit(solution)/shard_map/all_gather | solution.py:10
  334.9 14.4 %fusion = bf16[1024,896]{0,1:T(8,128)(2,1)} fusion(f32[896,1024]{1,0:T(8,128)} %fusion.19, bf16[4096,896]{1,0:T(8,128)(2,1)} %all-gather.5.cloned.1.call-done, bf16[1024,4096]{1,0:T(8,128)(2,1)} %bitcast.50), kind=kOutput, calls=%fused_computation.1 | convolution fusion | flops 7521697792 | bytes 21233664 | tf_op jit(solution)/shard_map/dot_general | solution.py:8
  349.3 0.0 copy-start.2
  349.3 3.1 copy.15
  352.4 0.0 copy-done.2
  352.4 0.0 copy-start.3
  352.4 1.9 fusion.11
  354.3 31.4 %all-reduce.10 = (bf16[1024,16]{0,1:T(8,128)(2,1)S(1)}, bf16[1024,16]{0,1:T(8,128)(2,1)S(1)}) all-reduce(f32[1024,16]{0,1:T(8,128)S(1)} %broadcast_multiply_fusion.1, f32[1024,16]{0,1:T(8,128)S(1)} %fusion.11), channel_id=1, replica_groups=mesh['dp'=2,'seq'=4,'tensor'=4] {'dp','tensor'}, use_global_device_ids=true, to_apply=%region_0.1 | all-reduce | flops 32768 | bytes 196608 | tf_op jit(solution)/shard_map/psum | solution.py:50
  385.6 1.0 fusion.8
  386.6 0.9 fusion.4
  387.5 0.0 all-reduce.9.cloned.1.call-update
  387.6 0.0 all-reduce.7.cloned.1.call-start
  387.6 40.4 %all-reduce.9.cloned.1.call-done = (f32[2,16,896]{2,1,0:T(8,128)}, f32[16,1024]{1,0:T(8,128)}) async-done(((f32[2,16,896]{2,1,0:T(8,128)}, f32[16,1024]{1,0:T(8,128)}), (f32[2,16,896]{2,1,0:T(8,128)}, f32[16,1024]{1,0:T(8,128)})) %all-reduce.9.cloned.1.call-update) | async-done | bytes 180240 | tf_op jit(solution)/shard_map/psum | solution.py:61
  428.0 1.5 multiply_reduce_fusion.2
  429.5 0.6 fusion.15
  430.1 1.0 multiply_reduce_fusion.1
  431.2 0.0 copy-done.3
  431.2 0.6 fusion.18
  431.7 11.7 %all-reduce.1 = (f32[2]{0:T(128)S(1)}, f32[2]{0:T(128)S(1)}) all-reduce(f32[2]{0:T(128)S(1)} %multiply_reduce_fusion.1, f32[2]{0:T(128)S(1)} %fusion.15), channel_id=1, replica_groups=mesh['dp'=2,'seq'=4,'tensor'=4] {'tensor'}, use_global_device_ids=true, to_apply=%region_3.4 | all-reduce | flops 4 | bytes 32 | tf_op jit(solution)/shard_map/psum | solution.py:64
  443.4 1.3 fusion.17
  444.7 2.1 broadcast_multiply_fusion
  446.8 0.0 all-reduce.7.cloned.1.call-update
  446.8 2.5 psum.59
  449.3 0.7 add_divide_fusion
  450.0 1.0 multiply_reduce_fusion
  451.0 1.9 all_gather.19
  452.9 9.2 %all-reduce.7.cloned.1.call-done = f32[16,1024]{1,0:T(8,128)} async-done(((f32[16,1024]{1,0:T(8,128)}), f32[16,1024]{1,0:T(8,128)}) %all-reduce.7.cloned.1.call-update) | async-done | bytes 65552 | tf_op jit(solution)/shard_map/psum | solution.py:70
  462.1 0.6 copy.31
  462.7 1.5 copy.32
  (5 shorter events, 0.1 us)
Async XLA Ops:
  7.2 18.8 %copy-start = (bf16[1,512,1024]{2,1,0:T(8,128)(2,1)S(1)}, bf16[1,512,1024]{2,1,0:T(8,128)(2,1)}, u32[]{:S(2)}) copy-start(bf16[1,512,1024]{2,1,0:T(8,128)(2,1)} %param.8) | copy-start | bytes 3145732
  7.2 15.7 %all-gather.7.cloned.1.call-start = ((), (), s32[]{:S(2)}) async-start(), calls=%async_computation.1 | async-start | bytes 3145728 | tf_op jit(solution)/shard_map/all_gather | solution.py:39
  7.9 96.9 %all-gather.11.cloned.1.call-start = ((), (), s32[]{:S(2)}) async-start(), calls=%async_computation.3 | async-start | bytes 9175040 | tf_op jit(solution)/shard_map/all_gather | solution.py:15
  11.0 245.1 %all-gather.9.cloned.1.call-start = ((), (), s32[]{:S(2)}) async-start(), calls=%async_computation.2 | async-start | bytes 10485760 | tf_op jit(solution)/shard_map/all_gather | solution.py:40
  22.9 3.1 copy-start.1
  22.9 312.0 %all-gather.5.cloned.1.call-start = ((), (), s32[]{:S(2)}) async-start(), calls=%async_computation | async-start | bytes 9175040 | tf_op jit(solution)/shard_map/all_gather | solution.py:10
  25.8 402.2 %all-reduce.9.cloned.1.call-start = ((), (), s32[]{:S(2)}) async-start(), calls=%async_computation.5 | async-start | bytes 360448 | tf_op jit(solution)/shard_map/psum | solution.py:61
  349.3 3.1 copy-start.2
  352.4 78.8 %copy-start.3 = (f32[2]{0:T(128)S(1)}, f32[2]{0:T(128)}, u32[]{:S(2)}) copy-start(f32[2]{0:T(128)} %param.13) | copy-start | bytes 28
  387.6 74.5 %all-reduce.7.cloned.1.call-start = ((), (), s32[]{:S(2)}) async-start(), calls=%async_computation.4 | async-start | bytes 131072 | tf_op jit(solution)/shard_map/psum | solution.py:70
Sparse Core Ops, SparseCore 0:
  9.6 13.2 all-gather.6
  24.7 80.0 all-gather.10
  106.4 149.6 all-gather.8
  257.8 77.0 all-gather.4
  387.7 40.2 all-reduce.8
  447.0 15.0 all-reduce.6
where the time goes:
time: 472 us; the launch traced here: 471 us
  waiting for transfers between devices  357 us (76%)
  blocking collectives  47.4 us (10%)
  matrix products  32.2 us (7%)
  between operations  14.2 us (3%)
  local copies, waits for them, and re-layouts  11.8 us (2%)
  other arithmetic  8.19 us (2%)
    all_gather x1, waiting for transfers between devices, body(): features = lax.all_gather(paired, 'tensor', axis=2, tiled=True)  151 us
    all_gather x1, waiting for transfers between devices, project(): lax.all_gather(up_cols, 'seq', axis=0, tiled=True)  78.4 us
    all_gather x1, waiting for transfers between devices, project(): lax.all_gather(gate_cols, 'seq', axis=0, tiled=True)  65.2 us
    psum x1, waiting for transfers between devices, body(): grads_a, grad_b = lax.psum((grads_a, grad_b), 'seq')  40.4 us
    psum x1, blocking collectives, body(): low_sum, back_sum = lax.psum((order_portion, back_place), ('dp', 'tensor'))  31.4 us
    dot_general x1, matrix products, project(): jnp.dot(features, lax.all_gather(gate_cols, 'seq', axis=0, tiled=True), p...  14.4 us
    dot_general x1, matrix products, project(): jnp.dot(features, lax.all_gather(up_cols, 'seq', axis=0, tiled=True), pre...  13.7 us
    all_gather x1, waiting for transfers between devices, body(): paired = lax.all_gather(incoming_activations, 'dp', axis=0, tiled=True)  11.8 us
  transfers between devices with their start and end apart: 6, of which 6 were waited for; matrix products, arithmetic and copies ran while one was open for 5% of the time, Pallas kernels for 0%

commit v1 on v0

v1 whole, which is shorter than its diff:
```python
import functools

import jax
import jax.numpy as jnp
from jax import lax
from jax.experimental import pallas as pl
from jax.experimental.pallas import tpu as pltpu
from jax.sharding import PartitionSpec as P

F32 = jnp.float32
BF16 = jnp.bfloat16
CONTRACT_LAST = (((1,), (1,)), ((), ()))


def kernel(
    nd, ns, nt, chunks, tile,
    x_hbm, g_hbm, gate_hbm, up_hbm, narrow_hbm, widen_ref, limits_ref,
    out_a, out_b,
    xg, wbuf, acc, hid, gbuf, narrow, back_parts, low_send, low_parts,
    a_parts, b_parts, a_final, b_final, squares,
    local_sem, x_send, x_recv, w_send, w_recv, back_send, back_recv,
    lows_send, lows_recv, ab_send, ab_recv, fin_send, fin_recv, sq_send, sq_recv,
):
    d, s, t = lax.axis_index("dp"), lax.axis_index("seq"), lax.axis_index("tensor")
    rows, kx = x_hbm.shape[1:]
    kw = gate_hbm.shape[0]
    width = narrow.shape[1]
    rank = narrow.shape[0]
    kc = kw // chunks
    group = nd * nt
    mine = d * nt + t

    def at(dd, ss, tt):
        return {"dp": dd, "seq": ss, "tensor": tt}

    def remote(src, dst, ssem, rsem, where):
        return pltpu.make_async_remote_copy(
            src_ref=src, dst_ref=dst, send_sem=ssem, recv_sem=rsem,
            device_id=where, device_id_type=pl.DeviceIdType.MESH,
        )

    def peer(k):
        q = (mine + k) % group
        return q // nt, q % nt

    sent = []

    def push(*args):
        copy = remote(*args)
        copy.start()
        sent.append(copy)

    cols = pl.ds(pl.multiple_of(d * width, 128), width)
    own_rows = pl.ds(pl.multiple_of(d * rows, rows), rows)

    locals_ = [
        pltpu.make_async_copy(g_hbm.at[0], gbuf, local_sem.at[0]),
        pltpu.make_async_copy(narrow_hbm.at[:, cols], narrow, local_sem.at[1]),
        pltpu.make_async_copy(x_hbm.at[0], xg.at[t, own_rows], local_sem.at[2]),
        pltpu.make_async_copy(gate_hbm.at[:, cols], wbuf.at[s, :, pl.ds(0, width)], local_sem.at[3]),
        pltpu.make_async_copy(up_hbm.at[:, cols], wbuf.at[s, :, pl.ds(width, width)], local_sem.at[4]),
    ]
    for copy in locals_:
        copy.start()

    barrier = pltpu.get_barrier_semaphore()
    for k in range(1, group):
        dd, tt = peer(k)
        pl.semaphore_signal(barrier, inc=1, device_id=at(dd, s, tt), device_id_type=pl.DeviceIdType.MESH)
    for k in range(1, ns):
        pl.semaphore_signal(barrier, inc=1, device_id=at(d, (s + k) % ns, t), device_id_type=pl.DeviceIdType.MESH)
    pl.semaphore_wait(barrier, group - 1 + ns - 1)

    def w_slot(block, c, part):
        return wbuf.at[block, pl.ds(c * kc, kc), pl.ds(part * width, width)]

    def w_push(k, where, c):
        for part, ref in enumerate((gate_hbm, up_hbm)):
            push(ref.at[pl.ds(c * kc, kc), cols], w_slot(s, c, part), w_send.at[k, c, part],
                 w_recv.at[s, c, part], at(d, where, t))

    def w_wait(block, c):
        for part in range(2):
            slot = w_slot(block, c, part)
            remote(slot, slot, w_send.at[0, c, part], w_recv.at[block, c, part], at(d, s, t)).wait_recv()

    def w_relay(block, c, where):
        for part in range(2):
            slot = w_slot(block, c, part)
            push(slot, slot, w_send.at[2, c, part], w_recv.at[block, c, part], at(d, where, t))

    relayed = ns == 4
    half = chunks // 2
    if relayed:
        xn, yn, dg = s + 1 - 2 * (s % 2), (s + 2) % 4, 3 - s
        order = [xn, yn, dg]
        for i in range(chunks):
            w_push(0, xn, i)
            w_push(1, yn, (i + half) % chunks)
    else:
        order = [(s + k) % ns for k in range(1, ns)]
        for k, where in enumerate(order):
            for c in range(chunks):
                w_push(k, where, c)

    for k in range(1, nt):
        push(x_hbm.at[0], xg.at[t, own_rows], x_send.at[0, k], x_recv.at[t, d], at(d, s, (t + k) % nt))
    for k in range(1, nd):
        push(x_hbm.at[0], xg.at[t, own_rows], x_send.at[k, 0], x_recv.at[t, d], at((d + k) % nd, s, t))

    locals_[0].wait()
    back_parts[d, t] = lax.dot_general(widen_ref[...], gbuf[...], CONTRACT_LAST, preferred_element_type=F32)
    for k in range(1, group):
        dd, tt = peer(k)
        push(back_parts.at[d, t], back_parts.at[d, t], back_send.at[k], back_recv.at[d, t], at(dd, s, tt))

    acc[...] = jnp.zeros_like(acc)

    if relayed:
        for i in range(max(half, chunks - half)):
            if i < half:
                w_wait(xn, i)
                w_relay(xn, i, yn)
            if half + i < chunks:
                w_wait(yn, half + i)
                w_relay(yn, half + i, xn)

    def x_wait(block, doc):
        slot = xg.at[block, pl.ds(pl.multiple_of(doc * rows, rows), rows)]
        remote(slot, slot, x_send.at[0, 0], x_recv.at[block, doc], at(d, s, t)).wait_recv()

    for k in range(1, nt):
        block = (t + nt - k) % nt
        x_wait(block, d)
        for j in range(1, nd):
            push(xg.at[block, own_rows], xg.at[block, own_rows], x_send.at[j, k], x_recv.at[block, d],
                 at((d + j) % nd, s, t))
    for j in range(1, nd):
        for k in range(nt):
            x_wait((t + nt - k) % nt, (d + j) % nd)
    for copy in locals_[1:]:
        copy.wait()

    for k in range(1, group):
        dd, tt = peer(k)
        slot = back_parts.at[dd, tt]
        remote(slot, slot, back_send.at[0], back_recv.at[dd, tt], at(d, s, t)).wait_recv()
    back = [jnp.sum(back_parts[j], axis=0).astype(BF16) for j in range(nd)]

    tiles = (nd * rows) // tile

    def accumulate(block, c):
        start = block * kw + c * kc
        of, lane = start // kx, pl.multiple_of(start % kx, kc)
        w_rows = pl.ds(pl.multiple_of(c * kc, kc), kc)

        def step(i, carry):
            r = pl.ds(pl.multiple_of(i * tile, tile), tile)
            acc[r, :] += jnp.dot(xg[of, r, pl.ds(lane, kc)], wbuf[block, w_rows, :], preferred_element_type=F32)
            return carry

        lax.fori_loop(0, tiles, step, 0)

    def whole_block(block):
        def step(c, carry):
            accumulate(block, c)
            return carry

        lax.fori_loop(0, chunks, step, 0)

    whole_block(s)
    for n, block in enumerate(order):
        last = n == len(order) - 1
        if relayed and last:
            for i in range(max(half, chunks - half)):
                for c in ([i] if i < half else []) + ([half + i] if half + i < chunks else []):
                    w_wait(block, c)
                    accumulate(block, c)
        else:
            for c in range(chunks):
                if not relayed or (n == 0 and c >= half) or (n == 1 and c < half):
                    w_wait(block, c)
            whole_block(block)

    def hidden(i, carry):
        r = pl.ds(pl.multiple_of(i * tile, tile), tile)
        gate, up = acc[r, pl.ds(0, width)], acc[r, pl.ds(width, width)]
        hid[r, :] = (gate / (1.0 + jnp.exp(-gate)) * up).astype(BF16)
        return carry

    lax.fori_loop(0, tiles, hidden, 0)

    for j in range(nd):
        low_send[j] = lax.dot_general(narrow[...], hid[pl.ds(j * rows, rows), :], CONTRACT_LAST,
                                      preferred_element_type=F32)
    for k in range(1, group):
        dd, tt = peer(k)
        push(low_send.at[dd], low_parts.at[d, t], lows_send.at[k], lows_recv.at[d, t], at(dd, s, tt))
    low_parts[d, t] = low_send[d]

    def ab_push(parts, which):
        for k in range(1, ns):
            push(parts.at[s], parts.at[s], ab_send.at[which, k], ab_recv.at[which, s], at(d, (s + k) % ns, t))

    def ab_wait(parts, which):
        for k in range(1, ns):
            slot = parts.at[(s + k) % ns]
            remote(slot, slot, ab_send.at[which, 0], ab_recv.at[which, (s + k) % ns], at(d, s, t)).wait_recv()

    for j in range(nd):
        a_parts[s, pl.ds(j * rank, rank), :] = jnp.dot(
            back[j], hid[pl.ds(j * rows, rows), :], preferred_element_type=F32)
    ab_push(a_parts, 0)

    for k in range(1, group):
        dd, tt = peer(k)
        slot = low_parts.at[dd, tt]
        remote(slot, slot, lows_send.at[0], lows_recv.at[dd, tt], at(d, s, t)).wait_recv()
    low = jnp.sum(low_parts[...], axis=(0, 1)).astype(BF16)
    b_parts[s] = jnp.dot(low, gbuf[...], preferred_element_type=F32)
    ab_push(b_parts, 1)

    ab_wait(a_parts, 0)
    doc_a = jnp.sum(a_parts[...], axis=0)
    a_final[d] = doc_a

    def fin_push(ref, which):
        for k in range(1, nd):
            push(ref.at[d], ref.at[d], fin_send.at[which, k], fin_recv.at[which, d], at((d + k) % nd, s, t))

    def fin_wait(ref, which):
        for k in range(1, nd):
            slot = ref.at[(d + k) % nd]
            remote(slot, slot, fin_send.at[which, 0], fin_recv.at[which, (d + k) % nd], at(d, s, t)).wait_recv()

    fin_push(a_final, 0)
    ab_wait(b_parts, 1)
    doc_b = jnp.sum(b_parts[...], axis=0)
    b_final[d] = doc_b
    fin_push(b_final, 1)

    def total(v):
        return jnp.sum(jnp.sum(v * v, axis=0, keepdims=True), axis=1, keepdims=True)

    line = lax.broadcasted_iota(jnp.int32, squares.shape[2:], 0)
    own = jnp.where(line == nd, total(doc_b), 0.0)
    for j in range(nd):
        own = jnp.where(line == j, total(doc_a[j * rank:(j + 1) * rank]), own)
    squares[d, t] = own
    for k in range(1, group):
        dd, tt = peer(k)
        push(squares.at[d, t], squares.at[d, t], sq_send.at[k], sq_recv.at[d, t], at(dd, s, tt))
    for k in range(1, group):
        dd, tt = peer(k)
        slot = squares.at[dd, tt]
        remote(slot, slot, sq_send.at[0], sq_recv.at[dd, tt], at(d, s, t)).wait_recv()
    per_doc = jnp.sum(squares[...], axis=1)
    over_docs = jnp.sum(per_doc, axis=0)

    fin_wait(a_final, 0)
    fin_wait(b_final, 1)
    factor_a = [limits_ref[0] / (jnp.sqrt(over_docs[j:j + 1, 0:1]) + 0.01) for j in range(nd)]
    factor_b = [limits_ref[1] / (jnp.sqrt(per_doc[j, nd:nd + 1, 0:1]) + 0.01) for j in range(nd)]
    for part in range(nd):
        out_a[:, pl.ds(part * width, width)] = sum(
            factor_a[j] * a_final[part, pl.ds(j * rank, rank), :] for j in range(nd))
    out_b[...] = sum(factor_b[j] * b_final[j] for j in range(nd))

    for copy in sent:
        copy.wait_send()


def body(x, g, gate, up, narrower, widener, limits):
    nd, ns, nt = lax.axis_size("dp"), lax.axis_size("seq"), lax.axis_size("tensor")
    rows, kx = x.shape[1:]
    kw, full = gate.shape
    rank = narrower.shape[0]
    width = full // nd
    kc = min(kw, 256)
    chunks = kw // kc
    dma = pltpu.SemaphoreType.DMA
    lines = -(-(nd + 1) // 8) * 8
    any_, vmem, smem = (pl.BlockSpec(memory_space=m) for m in (pl.ANY, pltpu.VMEM, pltpu.SMEM))
    return pl.pallas_call(
        functools.partial(kernel, nd, ns, nt, chunks, 256),
        out_shape=(
            jax.ShapeDtypeStruct((rank, full), F32),
            jax.ShapeDtypeStruct((rank, kx), F32),
        ),
        in_specs=[any_] * 5 + [vmem, smem],
        out_specs=(vmem, vmem),
        scratch_shapes=[
            pltpu.VMEM((nt, nd * rows, kx), BF16),
            pltpu.VMEM((ns, kw, 2 * width), BF16),
            pltpu.VMEM((nd * rows, 2 * width), F32),
            pltpu.VMEM((nd * rows, width), BF16),
            pltpu.VMEM((rows, kx), BF16),
            pltpu.VMEM((rank, width), BF16),
            pltpu.VMEM((nd, nt, rank, rows), F32),
            pltpu.VMEM((nd, rank, rows), F32),
            pltpu.VMEM((nd, nt, rank, rows), F32),
            pltpu.VMEM((ns, nd * rank, width), F32),
            pltpu.VMEM((ns, rank, kx), F32),
            pltpu.VMEM((nd, nd * rank, width), F32),
            pltpu.VMEM((nd, rank, kx), F32),
            pltpu.VMEM((nd, nt, lines, 128), F32),
            dma((5,)),
            dma((nd, nt)), dma((nt, nd)),
            dma((max(ns - 1, 3), chunks, 2)), dma((ns, chunks, 2)),
            dma((nd * nt,)), dma((nd, nt)),
            dma((nd * nt,)), dma((nd, nt)),
            dma((2, ns)), dma((2, ns)),
            dma((2, nd)), dma((2, nd)),
            dma((nd * nt,)), dma((nd, nt)),
        ],
        compiler_params=pltpu.CompilerParams(
            collective_id=0, has_side_effects=True, vmem_limit_bytes=56 * 2**20),
        name="adapter_gradients",
    )(x, g, gate, up, narrower, widener, limits)


def solution(mesh):
    in_specs = (
        P("dp", "seq", "tensor"),
        P("dp", "seq", "tensor"),
        P("seq", "tensor"),
        P("seq", "tensor"),
        P(None, "tensor"),
        P(None, "tensor"),
        P(),
    )
    out_specs = (P(None, "tensor"), P(None, "tensor"))
    return jax.shard_map(body, mesh=mesh, in_specs=in_specs, out_specs=out_specs, check_vma=False)
```

time: 472 us -> 155 us (0.33)
  waiting for transfers between devices: 357 us -> 0 us
  Pallas kernels: 0 us -> 151 us
  blocking collectives: 47.4 us -> 0 us
  matrix products: 32.2 us -> 0 us
  between operations: 14.2 us -> 0.64 us
  local copies, waits for them, and re-layouts: 11.8 us -> 3.02 us
  other arithmetic: 8.19 us -> 0 us
    all_gather x4 -> x0, waiting for transfers between devices: 307 us -> none  [the longest x1 151 us: body(): features = lax.all_gather(paired, 'tensor', axis=2, tiled=True)]
    pallas_call x0 -> x1, Pallas kernels: none -> 151 us  [body(): pl.pallas_call(functools.partial(kernel, nd, ns, nt, chunks, 256), out_sh...]
    psum x2 -> x0, waiting for transfers between devices: 49.7 us -> none  [the longest x1 40.4 us: body(): grads_a, grad_b = lax.psum((grads_a, grad_b), 'seq')]
    psum x3 -> x0, blocking collectives: 45.5 us -> none  [the longest x1 31.4 us: body(): low_sum, back_sum = lax.psum((order_portion, back_place), ('dp', 'tensor'))]
    dot_general x6 -> x0, matrix products: 32.2 us -> none  [the longest x1 14.4 us: project(): jnp.dot(features, lax.all_gather(gate_cols, 'seq', axis=0, tiled=True), p...]
    dynamic_slice x2 -> x0, local copies, waits for them, and re-layouts: 5.87 us -> none  [the longest x1 2.99 us: body(): lax.dynamic_slice_in_dim(fixed_raising_kernel, own * width, width, 1)]
    reduce_sum x4 -> x0, other arithmetic: 4.78 us -> none  [the longest x1 1.46 us: body(): squares_b = picker * jnp.sum(grad_b * grad_b)]
  transfers between devices with their start and end apart: 6 -> 0, of which waited for: 6 -> 0; matrix products, arithmetic and copies ran while one was open for 5% -> 0% of each run, Pallas kernels for 0% -> 0%
where the time goes in v1:
time: 155 us
  Pallas kernels  151 us (97%)
  local copies, waits for them, and re-layouts  3.02 us (2%)
    pallas_call x1, Pallas kernels, body(): pl.pallas_call(functools.partial(kernel, nd, ns, nt, chunks, 256), out_sh...  151 us

profile of v1, /device:TPU:0, one launch (start us, length us, event | category | flops | bytes accessed | tf_op | source)
XLA Modules:
  0.0 154.8 jit_solution(883963487202868125)
XLA Ops:
  0.6 151.1 %adapter_gradients.1 = (f32[16,1792]{1,0:T(8,128)}, f32[16,1024]{1,0:T(8,128)}) custom-call(bf16[1,512,1024]{2,1,0:T(8,128)(2,1)} %x_hbm.1, bf16[1,512,1024]{2,1,0:T(8,128)(2,1)} %g_hbm.1, bf16[1024,1792]{1,0:T(8,128)(2,1)} %gate_hbm.1, bf16[1024,1792]{1,0:T(8,128)(2,1)} %up_hbm.1, bf16[16,1792]{1,0:T(8,128)(2,1)} %narrow_hbm.1, bf16[16,1024]{1,0:T(8,128)(2,1)} %widen_ref.1, ...), custom_call_target="tpu_custom_call" | custom-call | tf_op jit(solution)/shard_map/adapter_gradients/pallas_call | solution.py:284
  151.7 1.6 %copy.11 = f32[16,1792]{1,0:T(8,128)} copy(f32[16,1792]{1,0:T(8,128)} %get-tuple-element.4) | data formatting | bytes 229376
  153.3 1.5 copy.12

commit v2 on v1

--- a/solution.py
+++ b/solution.py
@@ -276,7 +276,7 @@
     kw, full = gate.shape
     rank = narrower.shape[0]
     width = full // nd
-    kc = min(kw, 256)
+    kc = min(kw, 512)
     chunks = kw // kc
     dma = pltpu.SemaphoreType.DMA
     lines = -(-(nd + 1) // 8) * 8

time: 155 us -> 154 us (level)
  no operation moved by 1% of the time
where the time goes in v2:
time: 154 us
  Pallas kernels  150 us (97%)
  local copies, waits for them, and re-layouts  3.02 us (2%)
    pallas_call x1, Pallas kernels, body(): pl.pallas_call(functools.partial(kernel, nd, ns, nt, chunks, 256), out_sh...  150 us

profile of v2, /device:TPU:0, one launch (start us, length us, event | category | flops | bytes accessed | tf_op | source)
XLA Modules:
  0.0 153.9 jit_solution(6199916386488660976)
XLA Ops:
  0.6 150.2 %adapter_gradients.1 = (f32[16,1792]{1,0:T(8,128)}, f32[16,1024]{1,0:T(8,128)}) custom-call(bf16[1,512,1024]{2,1,0:T(8,128)(2,1)} %x_hbm.1, bf16[1,512,1024]{2,1,0:T(8,128)(2,1)} %g_hbm.1, bf16[1024,1792]{1,0:T(8,128)(2,1)} %gate_hbm.1, bf16[1024,1792]{1,0:T(8,128)(2,1)} %up_hbm.1, bf16[16,1792]{1,0:T(8,128)(2,1)} %narrow_hbm.1, bf16[16,1024]{1,0:T(8,128)(2,1)} %widen_ref.1, ...), custom_call_target="tpu_custom_call" | custom-call | tf_op jit(solution)/shard_map/adapter_gradients/pallas_call | solution.py:284
  150.9 1.6 %copy.11 = f32[16,1792]{1,0:T(8,128)} copy(f32[16,1792]{1,0:T(8,128)} %get-tuple-element.4) | data formatting | bytes 229376
  152.4 1.5 copy.12
